TPU v7x, 32 devices: a whole 2x2x4 slice. The times are simulated.
32 devices in a mesh: groups: 2 (over y), ep: 4 (over z), tp: 4 (over x, core).
Axes of the slice: x: 2, y: 2, z: 4, core: 2. Of those that a mesh axis runs over, the one named last changes fastest.
Arguments:
- latent_cache: bfloat16 [32, 576, 512], P(('groups', 'ep', 'tp')), parts along dimension 0, may hold values from -6 to 6
- queries: bfloat16 [32, 73728], P(('groups', 'ep'), 'tp'), parts along dimension 0, may hold values from -256 to 256
- destination: int32 [8, 4], P('groups'), parts along dimension 0, may hold values from 0 to 3, as said below
- cache_len: int32 [32], P(('groups', 'ep')), parts along dimension 0, may hold values from 64 to 512, as said below
- finished: int32 [32], P(('groups', 'ep')), parts along dimension 0, may hold values 0 or 1
- moe_input: bfloat16 [32, 7168], P(('groups', 'ep'), 'tp'), parts along dimension 0, may hold values from -6 to 6
- expert_ids: int32 [32, 8], P(('groups', 'ep')), parts along dimension 0, may hold values from 0 to 7, all different within a row; in each aligned block of 4 rows (0 to 3, 4 to 7, ...) at most 4 rows name the same one
- route_weight: bfloat16 [32, 8], P(('groups', 'ep')), parts along dimension 0, may hold values from 0.049804688 to 0.5
- up_weight: bfloat16 [8, 7168, 1024], P('ep', None, 'tp'), may hold values from -0.0625 to 0.0625
- down_weight: bfloat16 [8, 1024, 7168], P('ep', 'tp'), may hold values from -0.1875 to 0.1875
Outputs:
- moved_cache: bfloat16 [32, 576, 512], P(('groups', 'ep', 'tp')), parts along dimension 0
- context: bfloat16 [32, 65536], P(('groups', 'ep'), 'tp'), parts along dimension 0
- moe_out: bfloat16 [32, 7168], P(('groups', 'ep'), 'tp'), parts along dimension 0
There are 2 independent parts, one for each index of `groups`. A program takes and returns all parts, laid end to end along the dimension named above; an argument that names none is the same for every part. Nothing has to cross between parts.
Inputs may be any that keep to these rules, and one draw needn't show every extreme that they name: Each column destination[:, t] is a permutation of the replicas. `cache_len`: some request has exactly 512 valid positions. `expert_ids`: the 8 experts of a token differ; among the 4 tokens of one replica no expert is named more than 4 times, a bound that some block reaches.
All inputs are finite; a program needn't handle non-finite values. No bound on the sum of `finished` on one device may be relied on, other than what follows from the above.
Results may differ from a plain program's by a relative error of at most 0.02.
Values may be sent and summed in bfloat16 or wider, within the bound.
A program may use at most 64 MiB of HBM per device.

v0:
```python
import jax
import jax.numpy as jnp
from jax import lax
from jax.sharding import PartitionSpec as P

LATENT = 512
CAP = 4


score_scale = 192.0 ** (-0.5)


def attend_latent(query_block, caches, lengths, alive):
    scores = (
        jnp.einsum("nhc,ncp->nhp", query_block, caches, preferred_element_type=jnp.float32)
        * score_scale
    )
    positions = jnp.arange(caches.shape[2], dtype=jnp.int32)
    valid = positions[None, None, :] < lengths[:, None, None]
    scores = jnp.where(valid, scores, -jnp.inf)
    highest = jnp.max(scores, axis=2, keepdims=True)
    weights = jnp.exp(scores - highest)
    probabilities = (weights / jnp.sum(weights, axis=2, keepdims=True)).astype(jnp.bfloat16)
    attended = jnp.einsum(
        "nhp,ncp->nhc", probabilities, caches[:, :LATENT, :], preferred_element_type=jnp.float32
    )
    return jnp.where(alive[:, None, None], attended, 0.0).astype(jnp.bfloat16)


def shards(
    latent_cache,
    queries,
    destination,
    cache_len,
    finished,
    moe_input,
    expert_ids,
    route_weight,
    up_weight,
    down_weight,
):
    replicas = lax.axis_size("ep")
    slots = lax.axis_size("tp")
    slot_index = lax.axis_index("tp")
    latent_width = latent_cache.shape[1]
    length = latent_cache.shape[2]
    blocks = latent_cache.reshape(replicas, latent_width // replicas, length)
    spread = lax.all_to_all(blocks, "ep", split_axis=0, concat_axis=0, tiled=True)
    column = lax.dynamic_slice_in_dim(destination, slot_index, 1, 1)[:, 0]
    replica_ids = jnp.arange(replicas, dtype=jnp.int32)
    root = jnp.sum(
        jnp.where(column[:, None] == replica_ids[None, :], replica_ids[:, None], 0), axis=0
    )
    ordered = jnp.take(spread, root, axis=0)
    collected = lax.all_to_all(ordered, "ep", split_axis=0, concat_axis=0, tiled=True)
    moved_cache = collected.reshape(1, latent_width, length)
    alive = finished == 0
    arrived_queries = lax.all_to_all(queries, "tp", split_axis=0, concat_axis=1, tiled=True)
    heads_all = arrived_queries.shape[1] // latent_width
    own_length = lax.dynamic_slice_in_dim(cache_len, slot_index, 1, 0)
    own_alive = lax.dynamic_slice_in_dim(alive, slot_index, 1, 0)
    attended = attend_latent(
        arrived_queries.reshape(1, heads_all, latent_width), moved_cache, own_length, own_alive
    )
    context = lax.all_to_all(
        attended.reshape(1, heads_all * LATENT), "tp", split_axis=1, concat_axis=0, tiled=True
    )
    experts_local = up_weight.shape[0]
    experts = experts_local * replicas
    matches = expert_ids[:, :, None] == jnp.arange(experts, dtype=jnp.int32)[None, None, :]
    counts = jnp.sum(matches.astype(jnp.int32), axis=1) * alive[:, None].astype(jnp.int32)
    position = jnp.cumsum(counts, axis=0) - counts
    slot_hot = (position[:, :, None] == jnp.arange(CAP, dtype=jnp.int32)[None, None, :]) & (
        counts[:, :, None] > 0
    )
    dispatch = slot_hot.reshape(slots, experts * CAP).astype(jnp.bfloat16)
    weighting = jnp.sum(
        jnp.where(matches, route_weight[:, :, None].astype(jnp.float32), 0.0), axis=1
    )
    combine = (
        (slot_hot.astype(jnp.float32) * weighting[:, :, None])
        .reshape(slots, experts * CAP)
        .astype(jnp.bfloat16)
    )
    features = lax.all_gather(moe_input, "tp", axis=1, tiled=True)
    outgoing = jnp.einsum(
        "tq,td->qd", dispatch, features, preferred_element_type=jnp.float32
    ).astype(jnp.bfloat16)
    arrived = lax.all_to_all(
        outgoing.reshape(replicas, experts_local * CAP, features.shape[1]),
        "ep",
        split_axis=0,
        concat_axis=0,
        tiled=True,
    )
    arrived = arrived.reshape(replicas, experts_local, CAP, features.shape[1])
    raised = jnp.einsum("sjcd,jdh->sjch", arrived, up_weight, preferred_element_type=jnp.float32)
    hidden = jax.nn.silu(raised).astype(jnp.bfloat16)
    partial_terms = jnp.einsum(
        "sjch,jhd->sjcd", hidden, down_weight, preferred_element_type=jnp.float32
    )
    summed = lax.psum_scatter(
        partial_terms.astype(jnp.bfloat16), "tp", scatter_dimension=3, tiled=True
    )
    returned = lax.all_to_all(summed, "ep", split_axis=0, concat_axis=0, tiled=True)
    expert_rows = returned.reshape(experts * CAP, returned.shape[3])
    moe_out = jnp.dot(combine, expert_rows, preferred_element_type=jnp.float32).astype(jnp.bfloat16)
    return (moved_cache, context, moe_out)


def solution(mesh):
    return jax.shard_map(
        shards,
        mesh=mesh,
        in_specs=(
            P(("groups", "ep", "tp"), None, None),
            P(("groups", "ep"), "tp"),
            P("groups", None),
            P(("groups", "ep")),
            P(("groups", "ep")),
            P(("groups", "ep"), "tp"),
            P(("groups", "ep"), None),
            P(("groups", "ep"), None),
            P("ep", None, "tp"),
            P("ep", "tp", None),
        ),
        out_specs=(
            P(("groups", "ep", "tp"), None, None),
            P(("groups", "ep"), "tp"),
            P(("groups", "ep"), "tp"),
        ),
        check_vma=False,
    )
```

profile of v0, /device:TPU:0, one launch (start us, length us, event | category | flops | bytes accessed | tf_op | source)
XLA Modules:
  0.0 152.2 jit_solution(14776711041278752520)
XLA Ops:
  7.2 0.7 fusion.24
  7.8 0.8 convert_reduce_fusion
  8.8 0.1 and.32
  9.1 6.4 %all_gather.3 = bf16[4,7168]{1,0:T(4,128)(2,1)S(1)} all-gather(bf16[4,1792]{1,0:T(4,128)(2,1)} %param.15), channel_id=1, replica_groups=mesh['groups'=2,'ep'=4,'tp'=4] {'tp'}, dimensions={1}, use_global_device_ids=true | all-gather | bytes 71680 | tf_op jit(solution)/shard_map/all_gather | solution.py:85
  15.6 1.1 fusion
  16.7 5.3 %all-to-all-start.4 = ((bf16[4,8,7168]{2,1,0:T(8,128)(2,1)}), bf16[4,8,7168]{2,1,0:T(8,128)(2,1)S(1)}, u32[]{:S(2)}, u32[]{:S(2)}) async-start(bf16[4,8,7168]{2,1,0:T(8,128)(2,1)} %fusion), calls=%async_computation.4 | async-start | bytes 917504 | tf_op jit(solution)/shard_map/all_to_all | solution.py:89
  22.0 0.5 broadcast.167
  22.6 1.7 %reduce.9 = bf16[4,18432]{1,0:T(4,128)(2,1)S(1)} reduce(bf16[4,1,18432]{2,0,1:T(4,128)(2,1)} %bitcast.65, bf16[]{:T(256)} %broadcast.167), dimensions={1}, to_apply=%copy.25.reduce_sub_computation | reduce | bytes 294914 | tf_op jit(solution)/shard_map/all_to_all | solution.py:58
  24.3 0.8 reshape.230
  25.0 0.2 dynamic-slice_reduce_fusion
  25.2 0.1 select_reduce_fusion.1
  25.3 10.3 %all-to-all-done.4 = bf16[4,8,7168]{2,1,0:T(8,128)(2,1)S(1)} async-done(((bf16[4,8,7168]{2,1,0:T(8,128)(2,1)}), bf16[4,8,7168]{2,1,0:T(8,128)(2,1)S(1)}, u32[]{:S(2)}, u32[]{:S(2)}) %all-to-all-start.4) | async-done | bytes 458784 | tf_op jit(solution)/shard_map/all_to_all | solution.py:89
  35.6 3.5 %all-to-all-start = ((bf16[4,144,512]{2,1,0:T(8,128)(2,1)}), bf16[4,144,512]{2,1,0:T(8,128)(2,1)S(1)}, u32[]{:S(2)}, u32[]{:S(2)}) async-start(bf16[4,144,512]{2,1,0:T(8,128)(2,1)} %bitcast.63), calls=%async_computation | async-start | bytes 1179648 | tf_op jit(solution)/shard_map/all_to_all | solution.py:48
  39.2 0.4 copy.27
  39.5 4.5 %fusion.15 = bf16[4,2,4,256]{3,0,2,1:T(4,128)(2,1)S(1)} fusion(bf16[4,2,4,7168]{3,0,2,1:T(4,128)(2,1)S(1)} %bitcast.64, bf16[2,7168,256]{2,1,0:T(8,128)(2,1)} %param.18), kind=kOutput, calls=%fused_computation.23 | convolution fusion | flops 117481472 | bytes 7815168 | tf_op jit(solution)/shard_map/sjcd,jdh->sjch/dot_general | solution.py:97
  44.0 0.5 slice-done.1
  44.5 1.1 fusion.1
  45.6 15.3 %copy.32 = bf16[4,2,4,7168]{2,0,1,3:T(4,128)(2,1)} copy(bf16[4,2,4,7168]{3,2,0,1:T(4,128)(2,1)S(1)} %fusion.1) | data formatting | bytes 917504
  60.9 19.7 %reshape.226 = bf16[7168,32]{1,0:T(8,128)(2,1)} reshape(bf16[7168,2,4,4]{3,2,1,0:T(4,128)(2,1)} %bitcast.54) | data formatting | bytes 917504
  80.6 3.3 %all-to-all-start.2 = ((bf16[4,2,9216]{2,1,0:T(2,128)(2,1)}), bf16[4,2,9216]{2,1,0:T(2,128)(2,1)S(1)}, u32[]{:S(2)}, u32[]{:S(2)}) async-start(bf16[4,2,9216]{2,1,0:T(2,128)(2,1)} %reshape.230), calls=%async_computation.2 | async-start | bytes 294912 | tf_op jit(solution)/shard_map/all_to_all | solution.py:58
  84.0 0.6 gather_fusion
  84.6 0.9 broadcast_select_fusion
  85.5 3.2 %all-to-all-done.2 = bf16[4,2,9216]{2,1,0:T(2,128)(2,1)S(1)} async-done(((bf16[4,2,9216]{2,1,0:T(2,128)(2,1)}), bf16[4,2,9216]{2,1,0:T(2,128)(2,1)S(1)}, u32[]{:S(2)}, u32[]{:S(2)}) %all-to-all-start.2) | async-done | bytes 147488 | tf_op jit(solution)/shard_map/all_to_all | solution.py:58
  88.8 5.0 %all-to-all-start.1 = ((bf16[4,144,512]{2,1,0:T(8,128)(2,1)}), bf16[4,144,512]{2,1,0:T(8,128)(2,1)S(1)}, u32[]{:S(2)}, u32[]{:S(2)}) async-start(bf16[4,144,512]{2,1,0:T(8,128)(2,1)} %broadcast_select_fusion), calls=%async_computation.1 | async-start | bytes 1179648 | tf_op jit(solution)/shard_map/all_to_all | solution.py:55
  93.8 0.6 dynamic_slice.11
  94.3 0.6 dynamic_slice.10
  95.0 0.1 select_reduce_fusion
  95.2 0.1 convert_element_type.54
  95.2 0.7 iota_compare_fusion.2
  95.9 0.1 reshape.231
  96.0 0.9 reduce.7
  97.0 0.2 reshape.211
  97.2 14.8 %reduce-scatter.4.cloned.1.call-done = bf16[1792,32]{1,0:T(8,128)(2,1)} async-done(((bf16[7168,32]{1,0:T(8,128)(2,1)}), bf16[1792,32]{1,0:T(8,128)(2,1)}) %reduce-scatter.4.cloned.1.call-update) | async-done | bytes 114704
  111.9 7.3 %reshape.227 = bf16[1792,2,4,4]{3,2,1,0:T(4,128)(2,1)} reshape(bf16[1792,32]{1,0:T(8,128)(2,1)} %reduce-scatter.4.cloned.1.call-done) | data formatting | bytes 229376
  119.3 5.9 %copy.29 = bf16[4,2,4,1792]{3,2,1,0:T(4,128)(2,1)} copy(bf16[4,2,4,1792]{2,0,1,3:T(4,128)(2,1)} %bitcast.55) | data formatting | bytes 229376 | tf_op jit(solution)/shard_map/reduce_scatter | solution.py:102
  125.2 4.6 %all-to-all-start.5 = ((bf16[4,2,4,1792]{3,2,1,0:T(4,128)(2,1)}), bf16[4,2,4,1792]{3,2,1,0:T(4,128)(2,1)S(1)}, u32[]{:S(2)}, u32[]{:S(2)}) async-start(bf16[4,2,4,1792]{3,2,1,0:T(4,128)(2,1)} %copy.29), calls=%async_computation.5 | async-start | bytes 229376 | tf_op jit(solution)/shard_map/all_to_all | solution.py:105
  129.7 0.4 fusion.25
  130.1 0.1 fusion.10
  130.2 1.0 fusion.6
  131.3 1.5 reduce.10
  132.7 0.8 reshape.232
  133.6 2.1 %all-to-all-done.5 = bf16[4,2,4,1792]{3,2,1,0:T(4,128)(2,1)S(1)} async-done(((bf16[4,2,4,1792]{3,2,1,0:T(4,128)(2,1)}), bf16[4,2,4,1792]{3,2,1,0:T(4,128)(2,1)S(1)}, u32[]{:S(2)}, u32[]{:S(2)}) %all-to-all-start.5) | async-done | bytes 114720 | tf_op jit(solution)/shard_map/all_to_all | solution.py:105
  135.6 3.3 %all-to-all-start.3 = ((bf16[4,2,8192]{2,1,0:T(2,128)(2,1)}), bf16[4,2,8192]{2,1,0:T(2,128)(2,1)S(1)}, u32[]{:S(2)}, u32[]{:S(2)}) async-start(bf16[4,2,8192]{2,1,0:T(2,128)(2,1)} %reshape.232), calls=%async_computation.3 | async-start | bytes 262144 | tf_op jit(solution)/shard_map/all_to_all | solution.py:65
  139.0 0.7 convolution_convert_fusion.2
  139.7 3.8 %all-to-all-done.3 = bf16[4,2,8192]{2,1,0:T(2,128)(2,1)S(1)} async-done(((bf16[4,2,8192]{2,1,0:T(2,128)(2,1)}), bf16[4,2,8192]{2,1,0:T(2,128)(2,1)S(1)}, u32[]{:S(2)}, u32[]{:S(2)}) %all-to-all-start.3) | async-done | bytes 131104 | tf_op jit(solution)/shard_map/all_to_all | solution.py:65
  143.6 0.1 reshape.233
  143.7 0.8 copy.39
  144.5 0.8 copy.42
  (31 shorter events, 0.7 us)
Async XLA Ops:
  7.2 17.9 %copy-start = (s32[4,4]{1,0:T(4,128)S(1)}, s32[4,4]{1,0:T(4,128)}, u32[]{:S(2)}) copy-start(s32[4,4]{1,0:T(4,128)} %param.12) | copy-start | bytes 196
  16.7 18.9 %all-to-all-start.4 = ((bf16[4,8,7168]{2,1,0:T(8,128)(2,1)}), bf16[4,8,7168]{2,1,0:T(8,128)(2,1)S(1)}, u32[]{:S(2)}, u32[]{:S(2)}) async-start(bf16[4,8,7168]{2,1,0:T(8,128)(2,1)} %fusion), calls=%async_computation.4 | async-start | bytes 917504 | tf_op jit(solution)/shard_map/all_to_all | solution.py:89
  35.6 45.0 %all-to-all-start = ((bf16[4,144,512]{2,1,0:T(8,128)(2,1)}), bf16[4,144,512]{2,1,0:T(8,128)(2,1)S(1)}, u32[]{:S(2)}, u32[]{:S(2)}) async-start(bf16[4,144,512]{2,1,0:T(8,128)(2,1)} %bitcast.63), calls=%async_computation | async-start | bytes 1179648 | tf_op jit(solution)/shard_map/all_to_all | solution.py:48
  39.1 72.8 %reduce-scatter.4.cloned.1.call-start = ((), (), s32[]{:S(2)}) async-start(), calls=%async_computation.7 | async-start | bytes 2293760
  39.2 4.9 %slice-start = ((s8[7340032]{0:T(1024)(128)(4,1)}), s8[4194304]{0:T(1024)(128)(4,1)S(1)}, s32[]{:S(2)}) async-start(s8[7340032]{0:T(1024)(128)(4,1)} %bitcast.56), calls=%async_computation.8 | async-start | bytes 8388608
  39.5 5.0 %slice-start.1 = ((s8[7340032]{0:T(1024)(128)(4,1)}), s8[3145728]{0:T(1024)(128)(4,1)S(1)}, s32[]{:S(2)}) async-start(s8[7340032]{0:T(1024)(128)(4,1)} %bitcast.56), calls=%async_computation.9 | async-start | bytes 6291456
  60.8 32.9 %copy-start.3 = (s32[4]{0:T(128)S(1)}, s32[4]{0:T(128)}, u32[]{:S(2)}) copy-start(s32[4]{0:T(128)} %param.13) | copy-start | bytes 52
  60.8 34.1 %copy-start.2 = (bf16[4,8]{1,0:T(4,128)(2,1)S(1)}, bf16[4,8]{1,0:T(4,128)(2,1)}, u32[]{:S(2)}) copy-start(bf16[4,8]{1,0:T(4,128)(2,1)} %param.17) | copy-start | bytes 196
  60.9 34.1 %copy-start.1 = (s32[4,8]{1,0:T(4,128)S(1)}, s32[4,8]{1,0:T(4,128)}, u32[]{:S(2)}) copy-start(s32[4,8]{1,0:T(4,128)} %param.16) | copy-start | bytes 388
  80.6 8.1 %all-to-all-start.2 = ((bf16[4,2,9216]{2,1,0:T(2,128)(2,1)}), bf16[4,2,9216]{2,1,0:T(2,128)(2,1)S(1)}, u32[]{:S(2)}, u32[]{:S(2)}) async-start(bf16[4,2,9216]{2,1,0:T(2,128)(2,1)} %reshape.230), calls=%async_computation.2 | async-start | bytes 294912 | tf_op jit(solution)/shard_map/all_to_all | solution.py:58
  88.8 36.4 %all-to-all-start.1 = ((bf16[4,144,512]{2,1,0:T(8,128)(2,1)}), bf16[4,144,512]{2,1,0:T(8,128)(2,1)S(1)}, u32[]{:S(2)}, u32[]{:S(2)}) async-start(bf16[4,144,512]{2,1,0:T(8,128)(2,1)} %broadcast_select_fusion), calls=%async_computation.1 | async-start | bytes 1179648 | tf_op jit(solution)/shard_map/all_to_all | solution.py:55
  125.2 10.5 %all-to-all-start.5 = ((bf16[4,2,4,1792]{3,2,1,0:T(4,128)(2,1)}), bf16[4,2,4,1792]{3,2,1,0:T(4,128)(2,1)S(1)}, u32[]{:S(2)}, u32[]{:S(2)}) async-start(bf16[4,2,4,1792]{3,2,1,0:T(4,128)(2,1)} %copy.29), calls=%async_computation.5 | async-start | bytes 229376 | tf_op jit(solution)/shard_map/all_to_all | solution.py:105
  135.6 7.9 %all-to-all-start.3 = ((bf16[4,2,8192]{2,1,0:T(2,128)(2,1)}), bf16[4,2,8192]{2,1,0:T(2,128)(2,1)S(1)}, u32[]{:S(2)}, u32[]{:S(2)}) async-start(bf16[4,2,8192]{2,1,0:T(2,128)(2,1)} %reshape.232), calls=%async_computation.3 | async-start | bytes 262144 | tf_op jit(solution)/shard_map/all_to_all | solution.py:65
Sparse Core Ops, SparseCore 0:
  80.7 31.1 reduce-scatter.3
where the time goes:
time: 153 us; the launch traced here: 152 us
  local copies, waits for them, and re-layouts  55.8 us (36%)
  waiting for transfers between devices  34.2 us (22%)
  starting transfers between devices  25.1 us (16%)
  between operations  14.2 us (9%)
  matrix products  8.73 us (6%)
  other arithmetic  7.68 us (5%)
  blocking collectives  6.43 us (4%)
    unnamed x21, local copies, waits for them, and re-layouts  46.3 us
    unnamed x2, waiting for transfers between devices  14.8 us
    all_to_all x1, waiting for transfers between devices, shards(): lax.all_to_all(outgoing.reshape(replicas, experts_local * CAP, features.s...  10.3 us
    all_gather x1, blocking collectives, shards(): features = lax.all_gather(moe_input, 'tp', axis=1, tiled=True)  6.43 us
    reduce_scatter x1, local copies, waits for them, and re-layouts, shards(): lax.psum_scatter(partial_terms.astype(jnp.bfloat16), 'tp', scatter_dimens...  5.87 us
    all_to_all x1, starting transfers between devices, shards(): lax.all_to_all(outgoing.reshape(replicas, experts_local * CAP, features.s...  5.35 us
    all_to_all x1, starting transfers between devices, shards(): lax.all_to_all(ordered, 'ep', split_axis=0, concat_axis=0, tiled=True)  5.01 us
    all_to_all x1, starting transfers between devices, shards(): lax.all_to_all(summed, 'ep', split_axis=0, concat_axis=0, tiled=True)  4.59 us
  transfers between devices with their start and end apart: 7, of which 5 were waited for; matrix products, arithmetic and copies ran while one was open for 44% of the time, Pallas kernels for 0%

commit v1 on v0

v1 whole, which is shorter than its diff:
```python
import functools

import jax
import jax.numpy as jnp
from jax import lax
from jax.experimental import pallas as pl
from jax.experimental.pallas import tpu as pltpu
from jax.sharding import PartitionSpec as P

MESH = pl.DeviceIdType.MESH
LATENT = 512
LANES = 128
PACK = 16

score_scale = 192.0 ** (-0.5)


def when(condition, body):
    if condition is None:
        body()
    else:
        pl.when(condition)(body)


def layer_kernel(
    replicas,
    slots,
    chunk,
    destination,
    cache_len,
    finished,
    latent_cache,
    queries,
    moe_input,
    expert_ids,
    route_weight,
    up_weight,
    down_weight,
    moved_cache,
    context,
    moe_out,
    up_block,
    down_block,
    message,
    messages,
    tokens,
    features,
    spread,
    ordered,
    moved,
    own_queries,
    attended,
    partials,
    arrived,
    totals,
    shares,
    returned,
    local_sem,
    message_send,
    message_recv,
    spread_send,
    spread_recv,
    ordered_send,
    ordered_recv,
    feature_send,
    feature_recv,
    query_send,
    query_recv,
    context_send,
    context_recv,
    partial_send,
    partial_recv,
    share_send,
    share_recv,
):
    ep = lax.axis_index("ep")
    tp = lax.axis_index("tp")
    width = moe_input.shape[1]
    experts_local = up_weight.shape[0]
    carriers = latent_cache.shape[0] // chunk
    heads_total = own_queries.shape[0] * own_queries.shape[1]

    def carries(i):
        return None if carriers == replicas else i < carriers

    def forth(axis, me, count, k):
        return lax.rem(me + k, count)

    def back(axis, me, count, k):
        return lax.rem(me + count - k, count)

    def rows(i):
        return pl.ds(pl.multiple_of(i * chunk, PACK), chunk)

    def remote(src, dst, send, recv, axis, target):
        return pltpu.make_async_remote_copy(
            src_ref=src,
            dst_ref=dst,
            send_sem=send,
            recv_sem=recv,
            device_id={axis: target},
            device_id_type=MESH,
        )

    up_copy = pltpu.make_async_copy(up_weight, up_block, local_sem.at[0])
    down_copy = pltpu.make_async_copy(down_weight, down_block, local_sem.at[1])
    query_copy = pltpu.make_async_copy(queries.at[tp], own_queries.at[tp], local_sem.at[2])
    own_chunk = pltpu.make_async_copy(
        latent_cache.at[rows(ep if carriers == replicas else lax.rem(ep, carriers))],
        spread.at[ep],
        local_sem.at[3],
    )
    up_copy.start()
    down_copy.start()
    query_copy.start()
    own_chunk.start()

    lane = lax.broadcasted_iota(jnp.int32, (slots, LANES), 1)
    token = lax.broadcasted_iota(jnp.int32, (slots, LANES), 0)
    table = jnp.zeros((slots, LANES), jnp.float32)
    ids = expert_ids[...]
    weights = route_weight[...].astype(jnp.float32)
    for k in range(ids.shape[1]):
        table += jnp.where(ids[:, k : k + 1] == lane, weights[:, k : k + 1], 0.0)
    for s in range(slots):
        table = jnp.where((token == s) & (finished[s] != 0), 0.0, table)
    message[:, :width] = moe_input[...]
    message[:, width:] = table.astype(jnp.bfloat16)

    barrier = pltpu.get_barrier_semaphore()
    for k in range(1, replicas):
        pl.semaphore_signal(
            barrier, inc=1, device_id={"ep": lax.rem(ep + k, replicas)}, device_id_type=MESH
        )
    for k in range(1, slots):
        pl.semaphore_signal(
            barrier, inc=1, device_id={"tp": lax.rem(tp + k, slots)}, device_id_type=MESH
        )
    pl.semaphore_wait(barrier, replicas + slots - 2)

    def message_to(k):
        return remote(
            message, messages.at[ep], message_send.at[k], message_recv.at[k],
            "ep", lax.rem(ep + k, replicas),
        )

    def chunk_to(k):
        target = lax.rem(ep + k, replicas)
        return remote(
            latent_cache.at[rows(target)], spread.at[ep], spread_send.at[k], spread_recv.at[k],
            "ep", target,
        )

    def queries_to(k):
        target = lax.rem(tp + k, slots)
        return remote(
            queries.at[target], own_queries.at[tp], query_send.at[k], query_recv.at[k],
            "tp", target,
        )

    for k in range(1, replicas):
        message_to(k).start()
    for k in range(1, replicas):
        when(carries(lax.rem(ep + k, replicas)), lambda: chunk_to(k).start())
    for k in range(1, slots):
        queries_to(k).start()

    messages[ep] = message[...]
    for k in range(1, replicas):
        message_to(k).wait_recv()
    for r in range(replicas):
        tokens[r * slots : (r + 1) * slots, :] = messages[r].astype(jnp.float32)
    features[tp] = tokens[:, :width].astype(jnp.bfloat16)

    def features_to(k):
        return remote(
            features.at[tp], features.at[tp], feature_send.at[k], feature_recv.at[k],
            "tp", lax.rem(tp + k, slots),
        )

    for k in range(1, slots):
        features_to(k).start()

    def ordered_to(k):
        target = lax.rem(ep + k, replicas)
        return remote(
            ordered.at[target], moved.at[rows(ep)], ordered_send.at[k], ordered_recv.at[k],
            "ep", target,
        )

    def reorder():
        for k in range(1, replicas):
            chunk_to(k).wait_recv()
        def root_of(target):
            root = jnp.int32(0)
            for o in range(replicas):
                root = jnp.where(destination[o, tp] == target, jnp.int32(o), root)
            return root
        for k in range(1, replicas):
            target = lax.rem(ep + k, replicas)
            ordered[target] = spread[root_of(target)]
            ordered_to(k).start()
        moved[rows(ep), :] = spread[root_of(ep)]

    own_chunk.wait()
    when(carries(ep), reorder)

    for k in range(1, slots):
        features_to(k).wait_recv()
    up_copy.wait()
    down_copy.wait()
    all_weights = tokens[:, width:]
    all_lanes = lax.broadcasted_iota(jnp.int32, all_weights.shape, 1)
    weighted = []
    for j in range(experts_local):
        raised = None
        for t in range(slots):
            term = jnp.dot(
                features[t],
                up_block[j, t * width : (t + 1) * width, :],
                preferred_element_type=jnp.float32,
            )
            raised = term if raised is None else raised + term
        hidden = (raised / (1.0 + jnp.exp(-raised))).astype(jnp.bfloat16).astype(jnp.float32)
        column = jnp.sum(
            jnp.where(all_lanes == ep * experts_local + j, all_weights, 0.0), axis=1, keepdims=True
        )
        weighted.append((hidden * column).astype(jnp.bfloat16))
    for t in range(slots):
        total = None
        for j in range(experts_local):
            term = jnp.dot(
                weighted[j],
                down_block[j, :, t * width : (t + 1) * width],
                preferred_element_type=jnp.float32,
            )
            total = term if total is None else total + term
        partials[t] = total.astype(jnp.bfloat16)

    def partial_to(k):
        target = lax.rem(tp + k, slots)
        return remote(
            partials.at[target], arrived.at[tp], partial_send.at[k], partial_recv.at[k],
            "tp", target,
        )

    for k in range(1, slots):
        partial_to(k).start()

    totals[...] = partials[tp].astype(jnp.float32)
    for k in range(1, slots):
        partial_to(k).wait_recv()
        totals[...] += arrived[lax.rem(tp + slots - k, slots)].astype(jnp.float32)
    for r in range(replicas):
        shares[r] = totals[r * slots : (r + 1) * slots, :].astype(jnp.bfloat16)

    def share_to(k):
        target = lax.rem(ep + k, replicas)
        return remote(
            shares.at[target], returned.at[ep], share_send.at[k], share_recv.at[k],
            "ep", target,
        )

    for k in range(1, replicas):
        share_to(k).start()

    query_copy.wait()
    for k in range(1, slots):
        queries_to(k).wait_recv()
    for k in range(1, replicas):
        source = lax.rem(ep + replicas - k, replicas)
        arrival = remote(
            ordered.at[0], moved.at[rows(source)], ordered_send.at[k], ordered_recv.at[k],
            "ep", source,
        )
        when(carries(source), lambda: arrival.wait_recv())
    moved_copy = pltpu.make_async_copy(moved, moved_cache, local_sem.at[4])
    moved_copy.start()
    cache = moved[...]
    query_block = own_queries[...].reshape(heads_total, latent_cache.shape[0])
    scores = jnp.dot(query_block, cache, preferred_element_type=jnp.float32) * score_scale
    positions = lax.broadcasted_iota(jnp.int32, scores.shape, 1)
    scores = jnp.where(positions < cache_len[tp], scores, -jnp.inf)
    highest = jnp.max(scores, axis=1, keepdims=True)
    exps = jnp.exp(scores - highest)
    probabilities = (exps / jnp.sum(exps, axis=1, keepdims=True)).astype(jnp.bfloat16)
    result = lax.dot_general(
        probabilities, cache[:LATENT, :], (((1,), (1,)), ((), ())),
        preferred_element_type=jnp.float32,
    )
    result = jnp.where(finished[tp] == 0, result, 0.0).astype(jnp.bfloat16)
    attended[...] = result.reshape(attended.shape)

    def context_to(k):
        target = lax.rem(tp + k, slots)
        return remote(
            attended.at[target], context.at[tp], context_send.at[k], context_recv.at[k],
            "tp", target,
        )

    for k in range(1, slots):
        context_to(k).start()
    own_context = pltpu.make_async_copy(attended.at[tp], context.at[tp], local_sem.at[5])
    own_context.start()

    result = shares[ep].astype(jnp.float32)
    for k in range(1, replicas):
        share_to(k).wait_recv()
        result += returned[lax.rem(ep + replicas - k, replicas)].astype(jnp.float32)
    moe_out[...] = result.astype(jnp.bfloat16)

    for k in range(1, slots):
        context_to(k).wait_recv()
    own_context.wait()
    moved_copy.wait()
    for k in range(1, replicas):
        message_to(k).wait_send()
        share_to(k).wait_send()
        when(carries(lax.rem(ep + k, replicas)), lambda: chunk_to(k).wait_send())
        when(carries(ep), lambda: ordered_to(k).wait_send())
    for k in range(1, slots):
        queries_to(k).wait_send()
        features_to(k).wait_send()
        partial_to(k).wait_send()
        context_to(k).wait_send()


def shards(
    latent_cache,
    queries,
    destination,
    cache_len,
    finished,
    moe_input,
    expert_ids,
    route_weight,
    up_weight,
    down_weight,
):
    replicas = lax.axis_size("ep")
    slots = lax.axis_size("tp")
    latent_width, length = latent_cache.shape[1:]
    heads = queries.shape[1] // latent_width
    width = moe_input.shape[1]
    chunk = -(-(latent_width // replicas) // PACK) * PACK
    everyone = replicas * slots
    bf16, f32 = jnp.bfloat16, jnp.float32
    dma = pltpu.SemaphoreType.DMA
    anywhere = pl.BlockSpec(memory_space=pl.ANY)
    scalars = pl.BlockSpec(memory_space=pltpu.SMEM)
    near = pl.BlockSpec(memory_space=pltpu.VMEM)
    moved_cache, context, moe_out = pl.pallas_call(
        functools.partial(layer_kernel, replicas, slots, chunk),
        out_shape=(
            jax.ShapeDtypeStruct((latent_width, length), bf16),
            jax.ShapeDtypeStruct((slots, heads, LATENT), bf16),
            jax.ShapeDtypeStruct((slots, width), bf16),
        ),
        in_specs=[scalars] * 3 + [anywhere] * 2 + [near] * 3 + [anywhere] * 2,
        out_specs=(anywhere, anywhere, near),
        scratch_shapes=[
            pltpu.VMEM(up_weight.shape, bf16),
            pltpu.VMEM(down_weight.shape, bf16),
            pltpu.VMEM((slots, width + LANES), bf16),
            pltpu.VMEM((replicas, slots, width + LANES), bf16),
            pltpu.VMEM((everyone, width + LANES), f32),
            pltpu.VMEM((slots, everyone, width), bf16),
            pltpu.VMEM((replicas, chunk, length), bf16),
            pltpu.VMEM((replicas, chunk, length), bf16),
            pltpu.VMEM((latent_width, length), bf16),
            pltpu.VMEM((slots, heads, latent_width), bf16),
            pltpu.VMEM((slots, heads, LATENT), bf16),
            pltpu.VMEM((slots, everyone, width), bf16),
            pltpu.VMEM((slots, everyone, width), bf16),
            pltpu.VMEM((everyone, width), f32),
            pltpu.VMEM((replicas, slots, width), bf16),
            pltpu.VMEM((replicas, slots, width), bf16),
            dma((6,)),
            dma((replicas,)),
            dma((replicas,)),
            dma((replicas,)),
            dma((replicas,)),
            dma((replicas,)),
            dma((replicas,)),
            dma((slots,)),
            dma((slots,)),
            dma((slots,)),
            dma((slots,)),
            dma((slots,)),
            dma((slots,)),
            dma((slots,)),
            dma((slots,)),
            dma((replicas,)),
            dma((replicas,)),
        ],
        compiler_params=pltpu.CompilerParams(
            collective_id=0, has_side_effects=True, vmem_limit_bytes=44 * 1024 * 1024
        ),
    )(
        destination,
        cache_len,
        finished,
        latent_cache.reshape(latent_width, length),
        queries.reshape(slots, heads, latent_width),
        moe_input,
        expert_ids,
        route_weight,
        up_weight,
        down_weight,
    )
    return (
        moved_cache.reshape(1, latent_width, length),
        context.reshape(slots, heads * LATENT),
        moe_out,
    )


def solution(mesh):
    return jax.shard_map(
        shards,
        mesh=mesh,
        in_specs=(
            P(("groups", "ep", "tp"), None, None),
            P(("groups", "ep"), "tp"),
            P("groups", None),
            P(("groups", "ep")),
            P(("groups", "ep")),
            P(("groups", "ep"), "tp"),
            P(("groups", "ep"), None),
            P(("groups", "ep"), None),
            P("ep", None, "tp"),
            P("ep", "tp", None),
        ),
        out_specs=(
            P(("groups", "ep", "tp"), None, None),
            P(("groups", "ep"), "tp"),
            P(("groups", "ep"), "tp"),
        ),
        check_vma=False,
    )
```

time: 153 us -> 50.2 us (0.33)
  local copies, waits for them, and re-layouts: 55.8 us -> 11.5 us
  Pallas kernels: 0 us -> 37.1 us
  waiting for transfers between devices: 34.2 us -> 0 us
  starting transfers between devices: 25.1 us -> 0 us
  between operations: 14.2 us -> 0.66 us
  matrix products: 8.73 us -> 0 us
  other arithmetic: 7.68 us -> 0 us
  blocking collectives: 6.43 us -> 0 us
    pallas_call x0 -> x1, Pallas kernels: none -> 37.1 us  [shards(): pl.pallas_call(functools.partial(layer_kernel, replicas, slots, chunk), o...]
    unnamed x21 -> x19, local copies, waits for them, and re-layouts: 46.3 us -> 10.4 us
    all_to_all x6 -> x0, starting transfers between devices: 25.1 us -> none  [the longest x1 5.35 us: shards(): lax.all_to_all(outgoing.reshape(replicas, experts_local * CAP, features.s...]
    all_to_all x6 -> x0, waiting for transfers between devices: 19.4 us -> none  [the longest x1 10.3 us: shards(): lax.all_to_all(outgoing.reshape(replicas, experts_local * CAP, features.s...]
    unnamed x2 -> x0, waiting for transfers between devices: 14.8 us -> none
    dot_general x6 -> x0, matrix products: 8.73 us -> none  [the longest x1 4.46 us: shards(): jnp.einsum('sjcd,jdh->sjch', arrived, up_weight, preferred_element_type=j...]
    all_gather x1 -> x0, blocking collectives: 6.43 us -> none  [shards(): features = lax.all_gather(moe_input, 'tp', axis=1, tiled=True)]
    reduce_scatter x1 -> x0, local copies, waits for them, and re-layouts: 5.87 us -> none  [shards(): lax.psum_scatter(partial_terms.astype(jnp.bfloat16), 'tp', scatter_dimens...]
  transfers between devices with their start and end apart: 7 -> 0, of which waited for: 5 -> 0; matrix products, arithmetic and copies ran while one was open for 44% -> 0% of each run, Pallas kernels for 0% -> 0%
where the time goes in v1:
time: 50.2 us; the launch traced here: 49.2 us
  Pallas kernels  37.1 us (74%)
  local copies, waits for them, and re-layouts  11.5 us (23%)
  between operations  0.66 us (1%)
    pallas_call x1, Pallas kernels, shards(): pl.pallas_call(functools.partial(layer_kernel, replicas, slots, chunk), o...  37.1 us
    unnamed x19, local copies, waits for them, and re-layouts  10.4 us
    reshape x1, local copies, waits for them, and re-layouts, shards(): queries.reshape(slots, heads, latent_width)  1.11 us

profile of v1, /device:TPU:0, one launch (start us, length us, event | category | flops | bytes accessed | tf_op | source)
XLA Modules:
  0.0 49.2 jit_solution(4317876617991988144)
XLA Ops:
  0.6 1.1 %reshape.19.queries = bf16[4,32,576]{2,1,0:T(8,128)(2,1)S(1)} reshape(bf16[4,18432]{1,0:T(4,128)(2,1)} %param.11) | data formatting | bytes 294912 | tf_op jit(solution)/shard_map/reshape | solution.py:404
  1.7 0.0 copy-start
  1.8 3.1 %copy-done = bf16[2,7168,256]{2,1,0:T(8,128)(2,1)S(1)} copy-done((bf16[2,7168,256]{2,1,0:T(8,128)(2,1)S(1)}, bf16[2,7168,256]{2,1,0:T(8,128)(2,1)}, u32[]{:S(2)}) %copy-start) | copy-done | bytes 7340056
  4.8 0.0 copy-start.1
  4.8 1.1 %copy-done.1 = bf16[1,576,512]{2,1,0:T(8,128)(2,1)S(1)} copy-done((bf16[1,576,512]{2,1,0:T(8,128)(2,1)S(1)}, bf16[1,576,512]{2,1,0:T(8,128)(2,1)}, u32[]{:S(2)}) %copy-start.1) | copy-done | bytes 589848
  5.9 0.0 copy-start.2
  5.9 0.7 %copy-done.2 = bf16[4,1792]{1,0:T(4,128)(2,1)S(1)} copy-done((bf16[4,1792]{1,0:T(4,128)(2,1)S(1)}, bf16[4,1792]{1,0:T(4,128)(2,1)}, u32[]{:S(2)}) %copy-start.2) | copy-done | bytes 14360
  6.6 0.0 copy-start.3
  6.6 0.7 %copy-done.3 = s32[4,4]{1,0:T(4,128)S(1)} copy-done((s32[4,4]{1,0:T(4,128)S(1)}, s32[4,4]{1,0:T(4,128)}, u32[]{:S(2)}) %copy-start.3) | copy-done | bytes 88
  7.3 0.0 copy-start.4
  7.3 0.7 %copy-done.4 = s32[4,8]{1,0:T(4,128)S(1)} copy-done((s32[4,8]{1,0:T(4,128)S(1)}, s32[4,8]{1,0:T(4,128)}, u32[]{:S(2)}) %copy-start.4) | copy-done | bytes 152
  8.0 0.0 copy-start.5
  8.0 0.7 %copy-done.5 = bf16[4,8]{1,0:T(4,128)(2,1)S(1)} copy-done((bf16[4,8]{1,0:T(4,128)(2,1)S(1)}, bf16[4,8]{1,0:T(4,128)(2,1)}, u32[]{:S(2)}) %copy-start.5) | copy-done | bytes 88
  8.7 0.0 copy-start.6
  8.7 0.7 %copy-done.6 = s32[4]{0:T(128)S(1)} copy-done((s32[4]{0:T(128)S(1)}, s32[4]{0:T(128)}, u32[]{:S(2)}) %copy-start.6) | copy-done | bytes 40
  9.3 0.0 copy-start.7
  9.3 0.7 %copy-done.7 = s32[4]{0:T(128)S(1)} copy-done((s32[4]{0:T(128)S(1)}, s32[4]{0:T(128)}, u32[]{:S(2)}) %copy-start.7) | copy-done | bytes 40
  10.0 37.1 %shard_map.121 = (bf16[576,512]{1,0:T(8,128)(2,1)S(1)}, bf16[4,32,512]{2,1,0:T(8,128)(2,1)S(1)}, bf16[4,1792]{1,0:T(4,128)(2,1)S(1)}) custom-call(s32[4,4]{1,0:T(4,128)S(1)} %copy-done.3, s32[4]{0:T(128)S(1)} %copy-done.6, s32[4]{0:T(128)S(1)} %copy-done.7, bf16[576,512]{1,0:T(8,128)(2,1)S(1)} %bitcast.4, bf16[4,32,576]{2,1,0:T(8,128)(2,1)S(1)} %reshape.19.queries, ...), custom_call_target="tpu_custom_call" | custom-call | tf_op jit(solution)/shard_map/pallas_call | solution.py:352
  47.1 0.8 %copy.13 = bf16[1,4,32,512]{3,1,2,0:T(4,128)(2,1)} copy(bf16[1,4,32,512]{3,2,1,0:T(8,128)(2,1)S(1)} %bitcast.6) | data formatting | bytes 262144
  47.8 0.8 %copy.16 = bf16[1,576,512]{2,1,0:T(8,128)(2,1)} copy(bf16[1,576,512]{2,1,0:T(8,128)(2,1)S(1)} %bitcast.5) | data formatting | bytes 1179648
  48.6 0.6 %copy.17 = bf16[4,1792]{1,0:T(4,128)(2,1)} copy(bf16[4,1792]{1,0:T(4,128)(2,1)S(1)} %get-tuple-element.14) | data formatting | bytes 28672
Async XLA Ops:
  1.7 3.1 %copy-start = (bf16[2,7168,256]{2,1,0:T(8,128)(2,1)S(1)}, bf16[2,7168,256]{2,1,0:T(8,128)(2,1)}, u32[]{:S(2)}) copy-start(bf16[2,7168,256]{2,1,0:T(8,128)(2,1)} %up_weight.1) | copy-start | bytes 22020100
  4.8 1.1 %copy-start.1 = (bf16[1,576,512]{2,1,0:T(8,128)(2,1)S(1)}, bf16[1,576,512]{2,1,0:T(8,128)(2,1)}, u32[]{:S(2)}) copy-start(bf16[1,576,512]{2,1,0:T(8,128)(2,1)} %param.10) | copy-start | bytes 1769476
  5.9 0.7 %copy-start.2 = (bf16[4,1792]{1,0:T(4,128)(2,1)S(1)}, bf16[4,1792]{1,0:T(4,128)(2,1)}, u32[]{:S(2)}) copy-start(bf16[4,1792]{1,0:T(4,128)(2,1)} %moe_input.1) | copy-start | bytes 43012
  6.6 0.7 %copy-start.3 = (s32[4,4]{1,0:T(4,128)S(1)}, s32[4,4]{1,0:T(4,128)}, u32[]{:S(2)}) copy-start(s32[4,4]{1,0:T(4,128)} %destination.1) | copy-start | bytes 196
  7.3 0.7 %copy-start.4 = (s32[4,8]{1,0:T(4,128)S(1)}, s32[4,8]{1,0:T(4,128)}, u32[]{:S(2)}) copy-start(s32[4,8]{1,0:T(4,128)} %expert_ids.1) | copy-start | bytes 388
  8.0 0.7 %copy-start.5 = (bf16[4,8]{1,0:T(4,128)(2,1)S(1)}, bf16[4,8]{1,0:T(4,128)(2,1)}, u32[]{:S(2)}) copy-start(bf16[4,8]{1,0:T(4,128)(2,1)} %route_weight.1) | copy-start | bytes 196
  8.7 0.7 %copy-start.6 = (s32[4]{0:T(128)S(1)}, s32[4]{0:T(128)}, u32[]{:S(2)}) copy-start(s32[4]{0:T(128)} %cache_len.1) | copy-start | bytes 52
  9.3 0.7 %copy-start.7 = (s32[4]{0:T(128)S(1)}, s32[4]{0:T(128)}, u32[]{:S(2)}) copy-start(s32[4]{0:T(128)} %finished.1) | copy-start | bytes 52

commit v2 on v1

--- a/solution.py
+++ b/solution.py
@@ -39,6 +39,12 @@
     moved_cache,
     context,
     moe_out,
+    plan,
+    lengths,
+    ended,
+    input_block,
+    id_block,
+    route_block,
     up_block,
     down_block,
     message,
@@ -102,6 +108,16 @@
             device_id_type=MESH,
         )
 
+    barrier = pltpu.get_barrier_semaphore()
+    for k in range(1, replicas):
+        pl.semaphore_signal(
+            barrier, inc=1, device_id={"ep": lax.rem(ep + k, replicas)}, device_id_type=MESH
+        )
+    for k in range(1, slots):
+        pl.semaphore_signal(
+            barrier, inc=1, device_id={"tp": lax.rem(tp + k, slots)}, device_id_type=MESH
+        )
+
     up_copy = pltpu.make_async_copy(up_weight, up_block, local_sem.at[0])
     down_copy = pltpu.make_async_copy(down_weight, down_block, local_sem.at[1])
     query_copy = pltpu.make_async_copy(queries.at[tp], own_queries.at[tp], local_sem.at[2])
@@ -110,33 +126,42 @@
         spread.at[ep],
         local_sem.at[3],
     )
-    up_copy.start()
-    down_copy.start()
+    small = [
+        pltpu.make_async_copy(src, dst, local_sem.at[6 + i])
+        for i, (src, dst) in enumerate(
+            (
+                (moe_input, input_block),
+                (expert_ids, id_block),
+                (route_weight, route_block),
+                (finished, ended),
+                (destination, plan),
+                (cache_len, lengths),
+            )
+        )
+    ]
+    for copy in small:
+        copy.start()
     query_copy.start()
     own_chunk.start()
 
     lane = lax.broadcasted_iota(jnp.int32, (slots, LANES), 1)
     token = lax.broadcasted_iota(jnp.int32, (slots, LANES), 0)
     table = jnp.zeros((slots, LANES), jnp.float32)
-    ids = expert_ids[...]
-    weights = route_weight[...].astype(jnp.float32)
+    for copy in small:
+        copy.wait()
+    ids = id_block[...]
+    weights = route_block[...].astype(jnp.float32)
     for k in range(ids.shape[1]):
         table += jnp.where(ids[:, k : k + 1] == lane, weights[:, k : k + 1], 0.0)
     for s in range(slots):
-        table = jnp.where((token == s) & (finished[s] != 0), 0.0, table)
-    message[:, :width] = moe_input[...]
+        table = jnp.where((token == s) & (ended[s] != 0), 0.0, table)
+    message[:, :width] = input_block[...]
     message[:, width:] = table.astype(jnp.bfloat16)
 
-    barrier = pltpu.get_barrier_semaphore()
-    for k in range(1, replicas):
-        pl.semaphore_signal(
-            barrier, inc=1, device_id={"ep": lax.rem(ep + k, replicas)}, device_id_type=MESH
-        )
-    for k in range(1, slots):
-        pl.semaphore_signal(
-            barrier, inc=1, device_id={"tp": lax.rem(tp + k, slots)}, device_id_type=MESH
-        )
     pl.semaphore_wait(barrier, replicas + slots - 2)
+
+    up_copy.start()
+    down_copy.start()
 
     def message_to(k):
         return remote(
@@ -194,7 +219,7 @@
         def root_of(target):
             root = jnp.int32(0)
             for o in range(replicas):
-                root = jnp.where(destination[o, tp] == target, jnp.int32(o), root)
+                root = jnp.where(plan[o, tp] == target, jnp.int32(o), root)
             return root
         for k in range(1, replicas):
             target = lax.rem(ep + k, replicas)
@@ -280,7 +305,7 @@
     query_block = own_queries[...].reshape(heads_total, latent_cache.shape[0])
     scores = jnp.dot(query_block, cache, preferred_element_type=jnp.float32) * score_scale
     positions = lax.broadcasted_iota(jnp.int32, scores.shape, 1)
-    scores = jnp.where(positions < cache_len[tp], scores, -jnp.inf)
+    scores = jnp.where(positions < lengths[tp], scores, -jnp.inf)
     highest = jnp.max(scores, axis=1, keepdims=True)
     exps = jnp.exp(scores - highest)
     probabilities = (exps / jnp.sum(exps, axis=1, keepdims=True)).astype(jnp.bfloat16)
@@ -288,7 +313,7 @@
         probabilities, cache[:LATENT, :], (((1,), (1,)), ((), ())),
         preferred_element_type=jnp.float32,
     )
-    result = jnp.where(finished[tp] == 0, result, 0.0).astype(jnp.bfloat16)
+    result = jnp.where(ended[tp] == 0, result, 0.0).astype(jnp.bfloat16)
     attended[...] = result.reshape(attended.shape)
 
     def context_to(k):
@@ -347,7 +372,7 @@
     bf16, f32 = jnp.bfloat16, jnp.float32
     dma = pltpu.SemaphoreType.DMA
     anywhere = pl.BlockSpec(memory_space=pl.ANY)
-    scalars = pl.BlockSpec(memory_space=pltpu.SMEM)
+    far = pl.BlockSpec(memory_space=pltpu.HBM)
     near = pl.BlockSpec(memory_space=pltpu.VMEM)
     moved_cache, context, moe_out = pl.pallas_call(
         functools.partial(layer_kernel, replicas, slots, chunk),
@@ -356,9 +381,15 @@
             jax.ShapeDtypeStruct((slots, heads, LATENT), bf16),
             jax.ShapeDtypeStruct((slots, width), bf16),
         ),
-        in_specs=[scalars] * 3 + [anywhere] * 2 + [near] * 3 + [anywhere] * 2,
+        in_specs=[far] * 10,
         out_specs=(anywhere, anywhere, near),
         scratch_shapes=[
+            pltpu.SMEM(destination.shape, jnp.int32),
+            pltpu.SMEM(cache_len.shape, jnp.int32),
+            pltpu.SMEM(finished.shape, jnp.int32),
+            pltpu.VMEM(moe_input.shape, bf16),
+            pltpu.VMEM(expert_ids.shape, jnp.int32),
+            pltpu.VMEM(route_weight.shape, bf16),
             pltpu.VMEM(up_weight.shape, bf16),
             pltpu.VMEM(down_weight.shape, bf16),
             pltpu.VMEM((slots, width + LANES), bf16),
@@ -375,7 +406,7 @@
             pltpu.VMEM((everyone, width), f32),
             pltpu.VMEM((replicas, slots, width), bf16),
             pltpu.VMEM((replicas, slots, width), bf16),
-            dma((6,)),
+            dma((12,)),
             dma((replicas,)),
             dma((replicas,)),
             dma((replicas,)),
@@ -394,7 +425,7 @@
             dma((replicas,)),
         ],
         compiler_params=pltpu.CompilerParams(
-            collective_id=0, has_side_effects=True, vmem_limit_bytes=44 * 1024 * 1024
+            collective_id=0, has_side_effects=True, vmem_limit_bytes=56 * 1024 * 1024
         ),
     )(
         destination,

time: 50.2 us -> 44.6 us (0.89)
  the two profiles are of different devices: /device:TPU:0 before, /device:TPU:9 now
where the time goes in v2:
time: 44.6 us; the launch traced here: 44.3 us
  Pallas kernels  36.9 us (83%)
  local copies, waits for them, and re-layouts  6.68 us (15%)
  between operations  0.64 us (1%)
    pallas_call x1, Pallas kernels, shards(): pl.pallas_call(functools.partial(layer_kernel, replicas, slots, chunk), o...  36.9 us
    unnamed x3, local copies, waits for them, and re-layouts  4.9 us
    reshape x1, local copies, waits for them, and re-layouts, shards(): queries.reshape(slots, heads, latent_width)  1.78 us

profile of v2, /device:TPU:9, one launch (start us, length us, event | category | flops | bytes accessed | tf_op | source)
XLA Modules:
  0.0 44.3 jit_solution(4801311758428427730)
XLA Ops:
  0.6 1.8 %reshape.19.queries = bf16[4,32,576]{2,1,0:T(8,128)(2,1)} reshape(bf16[4,18432]{1,0:T(4,128)(2,1)} %param.11) | data formatting | bytes 294912 | tf_op jit(solution)/shard_map/reshape | solution.py:435
  2.4 36.9 %shard_map.121 = (bf16[576,512]{1,0:T(8,128)(2,1)}, bf16[4,32,512]{2,1,0:T(8,128)(2,1)}, bf16[4,1792]{1,0:T(4,128)(2,1)}) custom-call(s32[4,4]{1,0:T(4,128)} %destination.1, s32[4]{0:T(128)} %cache_len.1, s32[4]{0:T(128)} %finished.1, bf16[576,512]{1,0:T(8,128)(2,1)} %bitcast.4, bf16[4,32,576]{2,1,0:T(8,128)(2,1)} %reshape.19.queries, ...), custom_call_target="tpu_custom_call" | custom-call | tf_op jit(solution)/shard_map/pallas_call | solution.py:377
  39.4 1.7 %copy.13 = bf16[1,4,32,512]{3,1,2,0:T(4,128)(2,1)} copy(bf16[1,4,32,512]{3,2,1,0:T(8,128)(2,1)} %bitcast.7) | data formatting | bytes 262144
  41.0 1.9 %copy.16 = bf16[1,576,512]{2,1,0:T(8,128)(2,1)} copy(bf16[1,576,512]{2,1,0:T(8,128)(2,1)} %bitcast.5) | data formatting | bytes 1179648
  42.9 1.3 %copy.17 = bf16[4,1792]{1,0:T(4,128)(2,1)} copy(bf16[4,1792]{1,0:T(4,128)(2,1)} %get-tuple-element.14) | data formatting | bytes 28672

commit v3 on v2

--- a/solution.py
+++ b/solution.py
@@ -11,6 +11,7 @@
 LATENT = 512
 LANES = 128
 PACK = 16
+VMEM_BYTES = 56 * 1024 * 1024
 
 score_scale = 192.0 ** (-0.5)
 
@@ -26,6 +27,7 @@
     replicas,
     slots,
     chunk,
+    piece,
     destination,
     cache_len,
     finished,
@@ -54,6 +56,9 @@
     spread,
     ordered,
     moved,
+    query_rows,
+    query_heads,
+    sent_queries,
     own_queries,
     attended,
     partials,
@@ -61,7 +66,9 @@
     totals,
     shares,
     returned,
+    summed,
     local_sem,
+    own_sem,
     message_send,
     message_recv,
     spread_send,
@@ -84,6 +91,7 @@
     width = moe_input.shape[1]
     experts_local = up_weight.shape[0]
     carriers = latent_cache.shape[0] // chunk
+    pieces = chunk // piece
     heads_total = own_queries.shape[0] * own_queries.shape[1]
 
     def carries(i):
@@ -95,8 +103,11 @@
     def back(axis, me, count, k):
         return lax.rem(me + count - k, count)
 
-    def rows(i):
-        return pl.ds(pl.multiple_of(i * chunk, PACK), chunk)
+    def rows(i, p):
+        return pl.ds(pl.multiple_of(i * chunk + p * piece, PACK), piece)
+
+    def part(p):
+        return pl.ds(p * piece, piece)
 
     def remote(src, dst, send, recv, axis, target):
         return pltpu.make_async_remote_copy(
@@ -120,12 +131,15 @@
 
     up_copy = pltpu.make_async_copy(up_weight, up_block, local_sem.at[0])
     down_copy = pltpu.make_async_copy(down_weight, down_block, local_sem.at[1])
-    query_copy = pltpu.make_async_copy(queries.at[tp], own_queries.at[tp], local_sem.at[2])
-    own_chunk = pltpu.make_async_copy(
-        latent_cache.at[rows(ep if carriers == replicas else lax.rem(ep, carriers))],
-        spread.at[ep],
-        local_sem.at[3],
-    )
+    query_copy = pltpu.make_async_copy(queries, query_rows, local_sem.at[2])
+    own_chunk = [
+        pltpu.make_async_copy(
+            latent_cache.at[rows(ep if carriers == replicas else lax.rem(ep, carriers), p)],
+            spread[p].at[ep],
+            own_sem.at[p],
+        )
+        for p in range(pieces)
+    ]
     small = [
         pltpu.make_async_copy(src, dst, local_sem.at[6 + i])
         for i, (src, dst) in enumerate(
@@ -142,7 +156,8 @@
     for copy in small:
         copy.start()
     query_copy.start()
-    own_chunk.start()
+    for copy in own_chunk:
+        copy.start()
 
     lane = lax.broadcasted_iota(jnp.int32, (slots, LANES), 1)
     token = lax.broadcasted_iota(jnp.int32, (slots, LANES), 0)
@@ -169,24 +184,32 @@
             "ep", lax.rem(ep + k, replicas),
         )
 
-    def chunk_to(k):
+    def chunk_to(p, k):
         target = lax.rem(ep + k, replicas)
         return remote(
-            latent_cache.at[rows(target)], spread.at[ep], spread_send.at[k], spread_recv.at[k],
-            "ep", target,
+            latent_cache.at[rows(target, p)], spread[p].at[ep],
+            spread_send.at[p, k], spread_recv.at[p, k], "ep", target,
         )
 
     def queries_to(k):
         target = lax.rem(tp + k, slots)
         return remote(
-            queries.at[target], own_queries.at[tp], query_send.at[k], query_recv.at[k],
+            sent_queries.at[target], own_queries.at[tp], query_send.at[k], query_recv.at[k],
             "tp", target,
         )
 
     for k in range(1, replicas):
         message_to(k).start()
-    for k in range(1, replicas):
-        when(carries(lax.rem(ep + k, replicas)), lambda: chunk_to(k).start())
+    for p in range(pieces):
+        for k in range(1, replicas):
+            when(carries(lax.rem(ep + k, replicas)), lambda: chunk_to(p, k).start())
+
+    heads, latent = query_heads.shape[1:]
+    query_copy.wait()
+    for h in range(heads):
+        query_heads[:, h, :] = query_rows[:, h * latent : (h + 1) * latent].astype(jnp.float32)
+    sent_queries[...] = query_heads[...].astype(jnp.bfloat16)
+    own_queries[tp] = sent_queries[tp]
     for k in range(1, slots):
         queries_to(k).start()
 
@@ -206,38 +229,33 @@
     for k in range(1, slots):
         features_to(k).start()
 
-    def ordered_to(k):
+    def ordered_to(p, k):
         target = lax.rem(ep + k, replicas)
         return remote(
-            ordered.at[target], moved.at[rows(ep)], ordered_send.at[k], ordered_recv.at[k],
-            "ep", target,
-        )
-
-    def reorder():
+            ordered.at[target, part(p)], moved.at[rows(ep, p)],
+            ordered_send.at[p, k], ordered_recv.at[p, k], "ep", target,
+        )
+
+    def root_of(target):
+        root = jnp.int32(0)
+        for o in range(replicas):
+            root = jnp.where(plan[o, tp] == target, jnp.int32(o), root)
+        return root
+
+    def reorder(p):
         for k in range(1, replicas):
-            chunk_to(k).wait_recv()
-        def root_of(target):
-            root = jnp.int32(0)
-            for o in range(replicas):
-                root = jnp.where(plan[o, tp] == target, jnp.int32(o), root)
-            return root
+            chunk_to(p, k).wait_recv()
         for k in range(1, replicas):
             target = lax.rem(ep + k, replicas)
-            ordered[target] = spread[root_of(target)]
-            ordered_to(k).start()
-        moved[rows(ep), :] = spread[root_of(ep)]
-
-    own_chunk.wait()
-    when(carries(ep), reorder)
-
-    for k in range(1, slots):
-        features_to(k).wait_recv()
-    up_copy.wait()
-    down_copy.wait()
+            ordered[target, part(p), :] = spread[p][root_of(target)]
+            ordered_to(p, k).start()
+        moved[rows(ep, p), :] = spread[p][root_of(ep)]
+
     all_weights = tokens[:, width:]
     all_lanes = lax.broadcasted_iota(jnp.int32, all_weights.shape, 1)
     weighted = []
-    for j in range(experts_local):
+
+    def raise_tokens(j):
         raised = None
         for t in range(slots):
             term = jnp.dot(
@@ -251,6 +269,19 @@
             jnp.where(all_lanes == ep * experts_local + j, all_weights, 0.0), axis=1, keepdims=True
         )
         weighted.append((hidden * column).astype(jnp.bfloat16))
+
+    for p in range(pieces):
+        own_chunk[p].wait()
+        when(carries(ep), lambda: reorder(p))
+        if p == 0:
+            for k in range(1, slots):
+                features_to(k).wait_recv()
+            up_copy.wait()
+        if p < experts_local and p < pieces - 1:
+            raise_tokens(p)
+    for j in range(len(weighted), experts_local):
+        raise_tokens(j)
+    down_copy.wait()
     for t in range(slots):
         total = None
         for j in range(experts_local):
@@ -286,19 +317,18 @@
             "ep", target,
         )
 
+    for k in range(1, slots):
+        queries_to(k).wait_recv()
+    for p in range(pieces):
+        for k in range(1, replicas):
+            source = lax.rem(ep + replicas - k, replicas)
+            arrival = remote(
+                ordered.at[0, part(p)], moved.at[rows(source, p)],
+                ordered_send.at[p, k], ordered_recv.at[p, k], "ep", source,
+            )
+            when(carries(source), lambda: arrival.wait_recv())
     for k in range(1, replicas):
         share_to(k).start()
-
-    query_copy.wait()
-    for k in range(1, slots):
-        queries_to(k).wait_recv()
-    for k in range(1, replicas):
-        source = lax.rem(ep + replicas - k, replicas)
-        arrival = remote(
-            ordered.at[0], moved.at[rows(source)], ordered_send.at[k], ordered_recv.at[k],
-            "ep", source,
-        )
-        when(carries(source), lambda: arrival.wait_recv())
     moved_copy = pltpu.make_async_copy(moved, moved_cache, local_sem.at[4])
     moved_copy.start()
     cache = moved[...]
@@ -332,22 +362,40 @@
     for k in range(1, replicas):
         share_to(k).wait_recv()
         result += returned[lax.rem(ep + replicas - k, replicas)].astype(jnp.float32)
-    moe_out[...] = result.astype(jnp.bfloat16)
+    summed[...] = result.astype(jnp.bfloat16)
+    moe_copy = pltpu.make_async_copy(summed, moe_out, local_sem.at[12])
+    moe_copy.start()
 
     for k in range(1, slots):
         context_to(k).wait_recv()
     own_context.wait()
     moved_copy.wait()
+    moe_copy.wait()
     for k in range(1, replicas):
         message_to(k).wait_send()
         share_to(k).wait_send()
-        when(carries(lax.rem(ep + k, replicas)), lambda: chunk_to(k).wait_send())
-        when(carries(ep), lambda: ordered_to(k).wait_send())
+        for p in range(pieces):
+            when(carries(lax.rem(ep + k, replicas)), lambda: chunk_to(p, k).wait_send())
+            when(carries(ep), lambda: ordered_to(p, k).wait_send())
     for k in range(1, slots):
         queries_to(k).wait_send()
         features_to(k).wait_send()
         partial_to(k).wait_send()
         context_to(k).wait_send()
+
+
+def write_kernel(moved, attended, moe, moved_cache, context, moe_out, sem):
+    copies = [
+        pltpu.make_async_copy(moved, moved_cache, sem.at[0]),
+        pltpu.make_async_copy(moe, moe_out, sem.at[1]),
+    ]
+    for copy in copies:
+        copy.start()
+    rows = attended[...].astype(jnp.float32)
+    for h in range(rows.shape[1]):
+        context[:, h * LATENT : (h + 1) * LATENT] = rows[:, h, :].astype(jnp.bfloat16)
+    for copy in copies:
+        copy.wait()
 
 
 def shards(
@@ -368,6 +416,8 @@
     heads = queries.shape[1] // latent_width
     width = moe_input.shape[1]
     chunk = -(-(latent_width // replicas) // PACK) * PACK
+    piece = chunk // 3 if chunk % (3 * PACK) == 0 else chunk
+    pieces = chunk // piece
     everyone = replicas * slots
     bf16, f32 = jnp.bfloat16, jnp.float32
     dma = pltpu.SemaphoreType.DMA
@@ -375,14 +425,14 @@
     far = pl.BlockSpec(memory_space=pltpu.HBM)
     near = pl.BlockSpec(memory_space=pltpu.VMEM)
     moved_cache, context, moe_out = pl.pallas_call(
-        functools.partial(layer_kernel, replicas, slots, chunk),
+        functools.partial(layer_kernel, replicas, slots, chunk, piece),
         out_shape=(
             jax.ShapeDtypeStruct((latent_width, length), bf16),
             jax.ShapeDtypeStruct((slots, heads, LATENT), bf16),
             jax.ShapeDtypeStruct((slots, width), bf16),
         ),
         in_specs=[far] * 10,
-        out_specs=(anywhere, anywhere, near),
+        out_specs=(anywhere, anywhere, anywhere),
         scratch_shapes=[
             pltpu.SMEM(destination.shape, jnp.int32),
             pltpu.SMEM(cache_len.shape, jnp.int32),
@@ -396,9 +446,12 @@
             pltpu.VMEM((replicas, slots, width + LANES), bf16),
             pltpu.VMEM((everyone, width + LANES), f32),
             pltpu.VMEM((slots, everyone, width), bf16),
-            pltpu.VMEM((replicas, chunk, length), bf16),
+            [pltpu.VMEM((replicas, piece, length), bf16)] * pieces,
             pltpu.VMEM((replicas, chunk, length), bf16),
             pltpu.VMEM((latent_width, length), bf16),
+            pltpu.VMEM(queries.shape, bf16),
+            pltpu.VMEM((slots, heads, latent_width), f32),
+            pltpu.VMEM((slots, heads, latent_width), bf16),
             pltpu.VMEM((slots, heads, latent_width), bf16),
             pltpu.VMEM((slots, heads, LATENT), bf16),
             pltpu.VMEM((slots, everyone, width), bf16),
@@ -406,13 +459,15 @@
             pltpu.VMEM((everyone, width), f32),
             pltpu.VMEM((replicas, slots, width), bf16),
             pltpu.VMEM((replicas, slots, width), bf16),
-            dma((12,)),
+            pltpu.VMEM((slots, width), bf16),
+            dma((13,)),
+            dma((pieces,)),
             dma((replicas,)),
             dma((replicas,)),
-            dma((replicas,)),
-            dma((replicas,)),
-            dma((replicas,)),
-            dma((replicas,)),
+            dma((pieces, replicas)),
+            dma((pieces, replicas)),
+            dma((pieces, replicas)),
+            dma((pieces, replicas)),
             dma((slots,)),
             dma((slots,)),
             dma((slots,)),
@@ -425,25 +480,33 @@
             dma((replicas,)),
         ],
         compiler_params=pltpu.CompilerParams(
-            collective_id=0, has_side_effects=True, vmem_limit_bytes=56 * 1024 * 1024
+            collective_id=0, has_side_effects=True, vmem_limit_bytes=VMEM_BYTES
         ),
     )(
         destination,
         cache_len,
         finished,
         latent_cache.reshape(latent_width, length),
-        queries.reshape(slots, heads, latent_width),
+        queries,
         moe_input,
         expert_ids,
         route_weight,
         up_weight,
         down_weight,
     )
-    return (
-        moved_cache.reshape(1, latent_width, length),
-        context.reshape(slots, heads * LATENT),
-        moe_out,
-    )
+    moved_cache, context, moe_out = pl.pallas_call(
+        write_kernel,
+        out_shape=(
+            jax.ShapeDtypeStruct((latent_width, length), bf16),
+            jax.ShapeDtypeStruct((slots, heads * LATENT), bf16),
+            jax.ShapeDtypeStruct((slots, width), bf16),
+        ),
+        in_specs=[anywhere, near, anywhere],
+        out_specs=(far, near, far),
+        scratch_shapes=[dma((2,))],
+        compiler_params=pltpu.CompilerParams(vmem_limit_bytes=VMEM_BYTES),
+    )(moved_cache, context, moe_out)
+    return moved_cache.reshape(1, latent_width, length), context, moe_out
 
 
 def solution(mesh):

time: 44.6 us -> 60.3 us (1.35)
  the two profiles are of different devices: /device:TPU:9 before, /device:TPU:0 now
where the time goes in v3:
time: 60.3 us; the launch traced here: 60.1 us
  Pallas kernels  59.4 us (99%)
  between operations  0.64 us (1%)
    pallas_call x1, Pallas kernels, shards(): pl.pallas_call(functools.partial(layer_kernel, replicas, slots, chunk, pi...  38.4 us
    pallas_call x1, Pallas kernels, shards(): pl.pallas_call(write_kernel, out_shape=(jax.ShapeDtypeStruct((latent_widt...  21 us

profile of v3, /device:TPU:0, one launch (start us, length us, event | category | flops | bytes accessed | tf_op | source)
XLA Modules:
  0.0 60.1 jit_solution(4082475964735262535)
XLA Ops:
  0.6 38.4 %shard_map.121 = (bf16[576,512]{1,0:T(8,128)(2,1)}, bf16[4,32,512]{2,1,0:T(8,128)(2,1)}, bf16[4,1792]{1,0:T(4,128)(2,1)}) custom-call(s32[4,4]{1,0:T(4,128)} %destination.1, s32[4]{0:T(128)} %cache_len.1, s32[4]{0:T(128)} %finished.1, bf16[576,512]{1,0:T(8,128)(2,1)} %bitcast.2, bf16[4,18432]{1,0:T(4,128)(2,1)} %queries.1, bf16[4,1792]{1,0:T(4,128)(2,1)} %moe_input.1, ...), custom_call_target="tpu_custom_call" | custom-call | tf_op jit(solution)/shard_map/pallas_call | solution.py:427
  39.1 21.0 %shard_map.122 = (bf16[576,512]{1,0:T(8,128)(2,1)}, bf16[4,16384]{1,0:T(4,128)(2,1)}, bf16[4,1792]{1,0:T(4,128)(2,1)}) custom-call(bf16[576,512]{1,0:T(8,128)(2,1)} %get-tuple-element.9.moved, bf16[4,32,512]{2,1,0:T(8,128)(2,1)} %get-tuple-element.10.attended, bf16[4,1792]{1,0:T(4,128)(2,1)} %get-tuple-element.11.moe), custom_call_target="tpu_custom_call" | custom-call | tf_op jit(solution)/shard_map/pallas_call | solution.py:497

commit v4 on v3

--- a/solution.py
+++ b/solution.py
@@ -384,17 +384,36 @@
         context_to(k).wait_send()
 
 
-def write_kernel(moved, attended, moe, moved_cache, context, moe_out, sem):
-    copies = [
-        pltpu.make_async_copy(moved, moved_cache, sem.at[0]),
-        pltpu.make_async_copy(moe, moe_out, sem.at[1]),
+def write_kernel(
+    moved, attended, moe, moved_cache, context, moe_out, cache_block, rows_block, moe_block, line_block, sem
+):
+    parts = moved.shape[0] // 144
+    cuts = [pl.ds(i * 144, 144) for i in range(parts)]
+    rows_in = pltpu.make_async_copy(attended, rows_block, sem.at[0])
+    rows_out = pltpu.make_async_copy(line_block, context, sem.at[1])
+    moe_in = pltpu.make_async_copy(moe, moe_block, sem.at[2])
+    moe_back = pltpu.make_async_copy(moe_block, moe_out, sem.at[3])
+    cache_in = [
+        pltpu.make_async_copy(moved.at[cut], cache_block.at[cut], sem.at[4 + i])
+        for i, cut in enumerate(cuts)
     ]
-    for copy in copies:
+    cache_out = [
+        pltpu.make_async_copy(cache_block.at[cut], moved_cache.at[cut], sem.at[4 + parts + i])
+        for i, cut in enumerate(cuts)
+    ]
+    for copy in [rows_in] + cache_in + [moe_in]:
         copy.start()
-    rows = attended[...].astype(jnp.float32)
+    rows_in.wait()
+    rows = rows_block[...].astype(jnp.float32)
     for h in range(rows.shape[1]):
-        context[:, h * LATENT : (h + 1) * LATENT] = rows[:, h, :].astype(jnp.bfloat16)
-    for copy in copies:
+        line_block[:, h * LATENT : (h + 1) * LATENT] = rows[:, h, :].astype(jnp.bfloat16)
+    rows_out.start()
+    for arrived, leaving in zip(cache_in, cache_out):
+        arrived.wait()
+        leaving.start()
+    moe_in.wait()
+    moe_back.start()
+    for copy in cache_out + [rows_out, moe_back]:
         copy.wait()
 
 
@@ -423,7 +442,6 @@
     dma = pltpu.SemaphoreType.DMA
     anywhere = pl.BlockSpec(memory_space=pl.ANY)
     far = pl.BlockSpec(memory_space=pltpu.HBM)
-    near = pl.BlockSpec(memory_space=pltpu.VMEM)
     moved_cache, context, moe_out = pl.pallas_call(
         functools.partial(layer_kernel, replicas, slots, chunk, piece),
         out_shape=(
@@ -501,9 +519,15 @@
             jax.ShapeDtypeStruct((slots, heads * LATENT), bf16),
             jax.ShapeDtypeStruct((slots, width), bf16),
         ),
-        in_specs=[anywhere, near, anywhere],
-        out_specs=(far, near, far),
-        scratch_shapes=[dma((2,))],
+        in_specs=[anywhere] * 3,
+        out_specs=(far, far, far),
+        scratch_shapes=[
+            pltpu.VMEM((latent_width, length), bf16),
+            pltpu.VMEM((slots, heads, LATENT), bf16),
+            pltpu.VMEM((slots, width), bf16),
+            pltpu.VMEM((slots, heads * LATENT), bf16),
+            dma((4 + 2 * (latent_width // 144),)),
+        ],
         compiler_params=pltpu.CompilerParams(vmem_limit_bytes=VMEM_BYTES),
     )(moved_cache, context, moe_out)
     return moved_cache.reshape(1, latent_width, length), context, moe_out

time: 60.3 us -> 41.4 us (0.69)
  Pallas kernels: 59.4 us -> 40.5 us
    pallas_call x1, Pallas kernels: 21 us -> 2.02 us  [shards(): pl.pallas_call(write_kernel, out_shape=(jax.ShapeDtypeStruct((latent_widt...]
where the time goes in v4:
time: 41.4 us; the launch traced here: 41.1 us
  Pallas kernels  40.5 us (98%)
  between operations  0.64 us (2%)
    pallas_call x1, Pallas kernels, shards(): pl.pallas_call(functools.partial(layer_kernel, replicas, slots, chunk, pi...  38.4 us
    pallas_call x1, Pallas kernels, shards(): pl.pallas_call(write_kernel, out_shape=(jax.ShapeDtypeStruct((latent_widt...  2.02 us

profile of v4, /device:TPU:0, one launch (start us, length us, event | category | flops | bytes accessed | tf_op | source)
XLA Modules:
  0.0 41.1 jit_solution(266921785544896989)
XLA Ops:
  0.6 38.4 %shard_map.121 = (bf16[576,512]{1,0:T(8,128)(2,1)}, bf16[4,32,512]{2,1,0:T(8,128)(2,1)}, bf16[4,1792]{1,0:T(4,128)(2,1)}) custom-call(s32[4,4]{1,0:T(4,128)} %destination.1, s32[4]{0:T(128)} %cache_len.1, s32[4]{0:T(128)} %finished.1, bf16[576,512]{1,0:T(8,128)(2,1)} %bitcast.2, bf16[4,18432]{1,0:T(4,128)(2,1)} %queries.1, bf16[4,1792]{1,0:T(4,128)(2,1)} %moe_input.1, ...), custom_call_target="tpu_custom_call" | custom-call | tf_op jit(solution)/shard_map/pallas_call | solution.py:445
  39.1 2.0 %shard_map.122 = (bf16[576,512]{1,0:T(8,128)(2,1)}, bf16[4,16384]{1,0:T(4,128)(2,1)}, bf16[4,1792]{1,0:T(4,128)(2,1)}) custom-call(bf16[576,512]{1,0:T(8,128)(2,1)} %get-tuple-element.9.moved, bf16[4,32,512]{2,1,0:T(8,128)(2,1)} %get-tuple-element.10.attended, bf16[4,1792]{1,0:T(4,128)(2,1)} %get-tuple-element.11.moe), custom_call_target="tpu_custom_call" | custom-call | tf_op jit(solution)/shard_map/pallas_call | solution.py:515

commit v5 on v4

--- a/solution.py
+++ b/solution.py
@@ -11,6 +11,8 @@
 LATENT = 512
 LANES = 128
 PACK = 16
+PIECES = 3
+WINDOW = 3
 VMEM_BYTES = 56 * 1024 * 1024
 
 score_scale = 192.0 ** (-0.5)
@@ -21,6 +23,25 @@
         body()
     else:
         pl.when(condition)(body)
+
+
+def forth(me, count, k):
+    if count & (count - 1):
+        return lax.rem(me + k, count)
+    other, bit = me, 1
+    while bit < count:
+        if k & bit:
+            other = other + bit - 2 * bit * lax.rem(lax.div(me, bit), 2)
+        bit *= 2
+    return other
+
+
+def back(me, count, k):
+    return lax.rem(me + count - k, count) if count & (count - 1) else forth(me, count, k)
+
+
+def hops(count):
+    return list(range(count // 2, count)) + list(range(1, count // 2))
 
 
 def layer_kernel(
@@ -97,12 +118,6 @@
     def carries(i):
         return None if carriers == replicas else i < carriers
 
-    def forth(axis, me, count, k):
-        return lax.rem(me + k, count)
-
-    def back(axis, me, count, k):
-        return lax.rem(me + count - k, count)
-
     def rows(i, p):
         return pl.ds(pl.multiple_of(i * chunk + p * piece, PACK), piece)
 
@@ -120,13 +135,13 @@
         )
 
     barrier = pltpu.get_barrier_semaphore()
-    for k in range(1, replicas):
+    for k in hops(replicas):
         pl.semaphore_signal(
-            barrier, inc=1, device_id={"ep": lax.rem(ep + k, replicas)}, device_id_type=MESH
-        )
-    for k in range(1, slots):
+            barrier, inc=1, device_id={"ep": forth(ep, replicas, k)}, device_id_type=MESH
+        )
+    for k in hops(slots):
         pl.semaphore_signal(
-            barrier, inc=1, device_id={"tp": lax.rem(tp + k, slots)}, device_id_type=MESH
+            barrier, inc=1, device_id={"tp": forth(tp, slots, k)}, device_id_type=MESH
         )
 
     up_copy = pltpu.make_async_copy(up_weight, up_block, local_sem.at[0])
@@ -181,28 +196,31 @@
     def message_to(k):
         return remote(
             message, messages.at[ep], message_send.at[k], message_recv.at[k],
-            "ep", lax.rem(ep + k, replicas),
+            "ep", forth(ep, replicas, k),
         )
 
     def chunk_to(p, k):
-        target = lax.rem(ep + k, replicas)
+        target = forth(ep, replicas, k)
         return remote(
             latent_cache.at[rows(target, p)], spread[p].at[ep],
             spread_send.at[p, k], spread_recv.at[p, k], "ep", target,
         )
 
     def queries_to(k):
-        target = lax.rem(tp + k, slots)
+        target = forth(tp, slots, k)
         return remote(
             sent_queries.at[target], own_queries.at[tp], query_send.at[k], query_recv.at[k],
             "tp", target,
         )
 
-    for k in range(1, replicas):
+    for k in hops(replicas):
         message_to(k).start()
-    for p in range(pieces):
-        for k in range(1, replicas):
-            when(carries(lax.rem(ep + k, replicas)), lambda: chunk_to(p, k).start())
+    def send_piece(p):
+        for k in hops(replicas):
+            when(carries(forth(ep, replicas, k)), lambda: chunk_to(p, k).start())
+
+    for p in range(min(WINDOW, pieces)):
+        send_piece(p)
 
     heads, latent = query_heads.shape[1:]
     query_copy.wait()
@@ -210,11 +228,11 @@
         query_heads[:, h, :] = query_rows[:, h * latent : (h + 1) * latent].astype(jnp.float32)
     sent_queries[...] = query_heads[...].astype(jnp.bfloat16)
     own_queries[tp] = sent_queries[tp]
-    for k in range(1, slots):
+    for k in hops(slots):
         queries_to(k).start()
 
     messages[ep] = message[...]
-    for k in range(1, replicas):
+    for k in hops(replicas):
         message_to(k).wait_recv()
     for r in range(replicas):
         tokens[r * slots : (r + 1) * slots, :] = messages[r].astype(jnp.float32)
@@ -223,14 +241,14 @@
     def features_to(k):
         return remote(
             features.at[tp], features.at[tp], feature_send.at[k], feature_recv.at[k],
-            "tp", lax.rem(tp + k, slots),
-        )
-
-    for k in range(1, slots):
+            "tp", forth(tp, slots, k),
+        )
+
+    for k in hops(slots):
         features_to(k).start()
 
     def ordered_to(p, k):
-        target = lax.rem(ep + k, replicas)
+        target = forth(ep, replicas, k)
         return remote(
             ordered.at[target, part(p)], moved.at[rows(ep, p)],
             ordered_send.at[p, k], ordered_recv.at[p, k], "ep", target,
@@ -243,10 +261,10 @@
         return root
 
     def reorder(p):
-        for k in range(1, replicas):
+        for k in hops(replicas):
             chunk_to(p, k).wait_recv()
-        for k in range(1, replicas):
-            target = lax.rem(ep + k, replicas)
+        for k in hops(replicas):
+            target = forth(ep, replicas, k)
             ordered[target, part(p), :] = spread[p][root_of(target)]
             ordered_to(p, k).start()
         moved[rows(ep, p), :] = spread[p][root_of(ep)]
@@ -273,8 +291,10 @@
     for p in range(pieces):
         own_chunk[p].wait()
         when(carries(ep), lambda: reorder(p))
+        if p + WINDOW < pieces:
+            send_piece(p + WINDOW)
         if p == 0:
-            for k in range(1, slots):
+            for k in hops(slots):
                 features_to(k).wait_recv()
             up_copy.wait()
         if p < experts_local and p < pieces - 1:
@@ -294,41 +314,42 @@
         partials[t] = total.astype(jnp.bfloat16)
 
     def partial_to(k):
-        target = lax.rem(tp + k, slots)
+        target = forth(tp, slots, k)
         return remote(
             partials.at[target], arrived.at[tp], partial_send.at[k], partial_recv.at[k],
             "tp", target,
         )
 
-    for k in range(1, slots):
+    for k in hops(slots):
         partial_to(k).start()
 
     totals[...] = partials[tp].astype(jnp.float32)
-    for k in range(1, slots):
+    for k in hops(slots):
         partial_to(k).wait_recv()
-        totals[...] += arrived[lax.rem(tp + slots - k, slots)].astype(jnp.float32)
+        totals[...] += arrived[back(tp, slots, k)].astype(jnp.float32)
     for r in range(replicas):
         shares[r] = totals[r * slots : (r + 1) * slots, :].astype(jnp.bfloat16)
 
     def share_to(k):
-        target = lax.rem(ep + k, replicas)
+        target = forth(ep, replicas, k)
         return remote(
             shares.at[target], returned.at[ep], share_send.at[k], share_recv.at[k],
             "ep", target,
         )
 
-    for k in range(1, slots):
+    for k in hops(replicas):
+        share_to(k).start()
+
+    for k in hops(slots):
         queries_to(k).wait_recv()
     for p in range(pieces):
-        for k in range(1, replicas):
-            source = lax.rem(ep + replicas - k, replicas)
+        for k in hops(replicas):
+            source = back(ep, replicas, k)
             arrival = remote(
                 ordered.at[0, part(p)], moved.at[rows(source, p)],
                 ordered_send.at[p, k], ordered_recv.at[p, k], "ep", source,
             )
             when(carries(source), lambda: arrival.wait_recv())
-    for k in range(1, replicas):
-        share_to(k).start()
     moved_copy = pltpu.make_async_copy(moved, moved_cache, local_sem.at[4])
     moved_copy.start()
     cache = moved[...]
@@ -347,37 +368,37 @@
     attended[...] = result.reshape(attended.shape)
 
     def context_to(k):
-        target = lax.rem(tp + k, slots)
+        target = forth(tp, slots, k)
         return remote(
             attended.at[target], context.at[tp], context_send.at[k], context_recv.at[k],
             "tp", target,
         )
 
-    for k in range(1, slots):
+    for k in hops(slots):
         context_to(k).start()
     own_context = pltpu.make_async_copy(attended.at[tp], context.at[tp], local_sem.at[5])
     own_context.start()
 
     result = shares[ep].astype(jnp.float32)
-    for k in range(1, replicas):
+    for k in hops(replicas):
         share_to(k).wait_recv()
-        result += returned[lax.rem(ep + replicas - k, replicas)].astype(jnp.float32)
+        result += returned[back(ep, replicas, k)].astype(jnp.float32)
     summed[...] = result.astype(jnp.bfloat16)
     moe_copy = pltpu.make_async_copy(summed, moe_out, local_sem.at[12])
     moe_copy.start()
 
-    for k in range(1, slots):
+    for k in hops(slots):
         context_to(k).wait_recv()
     own_context.wait()
     moved_copy.wait()
     moe_copy.wait()
-    for k in range(1, replicas):
+    for k in hops(replicas):
         message_to(k).wait_send()
         share_to(k).wait_send()
         for p in range(pieces):
-            when(carries(lax.rem(ep + k, replicas)), lambda: chunk_to(p, k).wait_send())
+            when(carries(forth(ep, replicas, k)), lambda: chunk_to(p, k).wait_send())
             when(carries(ep), lambda: ordered_to(p, k).wait_send())
-    for k in range(1, slots):
+    for k in hops(slots):
         queries_to(k).wait_send()
         features_to(k).wait_send()
         partial_to(k).wait_send()
@@ -435,7 +456,7 @@
     heads = queries.shape[1] // latent_width
     width = moe_input.shape[1]
     chunk = -(-(latent_width // replicas) // PACK) * PACK
-    piece = chunk // 3 if chunk % (3 * PACK) == 0 else chunk
+    piece = chunk // PIECES if chunk % (PIECES * PACK) == 0 else chunk
     pieces = chunk // piece
     everyone = replicas * slots
     bf16, f32 = jnp.bfloat16, jnp.float32

time: 41.4 us -> 40.3 us (0.973)
  Pallas kernels: 40.5 us -> 39.4 us
    pallas_call x1, Pallas kernels: 38.4 us -> 37.4 us  [shards(): pl.pallas_call(functools.partial(layer_kernel, replicas, slots, chunk, pi...]
where the time goes in v5:
time: 40.3 us; the launch traced here: 40.1 us
  Pallas kernels  39.4 us (98%)
  between operations  0.64 us (2%)
    pallas_call x1, Pallas kernels, shards(): pl.pallas_call(functools.partial(layer_kernel, replicas, slots, chunk, pi...  37.4 us
    pallas_call x1, Pallas kernels, shards(): pl.pallas_call(write_kernel, out_shape=(jax.ShapeDtypeStruct((latent_widt...  2.02 us

profile of v5, /device:TPU:0, one launch (start us, length us, event | category | flops | bytes accessed | tf_op | source)
XLA Modules:
  0.0 40.1 jit_solution(7231307437698130413)
XLA Ops:
  0.6 37.4 %shard_map.121 = (bf16[576,512]{1,0:T(8,128)(2,1)}, bf16[4,32,512]{2,1,0:T(8,128)(2,1)}, bf16[4,1792]{1,0:T(4,128)(2,1)}) custom-call(s32[4,4]{1,0:T(4,128)} %destination.1, s32[4]{0:T(128)} %cache_len.1, s32[4]{0:T(128)} %finished.1, bf16[576,512]{1,0:T(8,128)(2,1)} %bitcast.2, bf16[4,18432]{1,0:T(4,128)(2,1)} %queries.1, bf16[4,1792]{1,0:T(4,128)(2,1)} %moe_input.1, ...), custom_call_target="tpu_custom_call" | custom-call | tf_op jit(solution)/shard_map/pallas_call | solution.py:466
  38.0 2.0 %shard_map.122 = (bf16[576,512]{1,0:T(8,128)(2,1)}, bf16[4,16384]{1,0:T(4,128)(2,1)}, bf16[4,1792]{1,0:T(4,128)(2,1)}) custom-call(bf16[576,512]{1,0:T(8,128)(2,1)} %get-tuple-element.9.moved, bf16[4,32,512]{2,1,0:T(8,128)(2,1)} %get-tuple-element.10.attended, bf16[4,1792]{1,0:T(4,128)(2,1)} %get-tuple-element.11.moe), custom_call_target="tpu_custom_call" | custom-call | tf_op jit(solution)/shard_map/pallas_call | solution.py:536

commit v6 on v5

--- a/solution.py
+++ b/solution.py
@@ -11,7 +11,6 @@
 LATENT = 512
 LANES = 128
 PACK = 16
-PIECES = 3
 WINDOW = 3
 VMEM_BYTES = 56 * 1024 * 1024
 
@@ -112,17 +111,16 @@
     width = moe_input.shape[1]
     experts_local = up_weight.shape[0]
     carriers = latent_cache.shape[0] // chunk
-    pieces = chunk // piece
-    heads_total = own_queries.shape[0] * own_queries.shape[1]
+    pieces = len(piece)
 
     def carries(i):
         return None if carriers == replicas else i < carriers
 
     def rows(i, p):
-        return pl.ds(pl.multiple_of(i * chunk + p * piece, PACK), piece)
+        return pl.ds(pl.multiple_of(i * chunk + sum(piece[:p]), PACK), piece[p])
 
     def part(p):
-        return pl.ds(p * piece, piece)
+        return pl.ds(sum(piece[:p]), piece[p])
 
     def remote(src, dst, send, recv, axis, target):
         return pltpu.make_async_remote_copy(
@@ -353,19 +351,22 @@
     moved_copy = pltpu.make_async_copy(moved, moved_cache, local_sem.at[4])
     moved_copy.start()
     cache = moved[...]
-    query_block = own_queries[...].reshape(heads_total, latent_cache.shape[0])
-    scores = jnp.dot(query_block, cache, preferred_element_type=jnp.float32) * score_scale
-    positions = lax.broadcasted_iota(jnp.int32, scores.shape, 1)
-    scores = jnp.where(positions < lengths[tp], scores, -jnp.inf)
-    highest = jnp.max(scores, axis=1, keepdims=True)
-    exps = jnp.exp(scores - highest)
-    probabilities = (exps / jnp.sum(exps, axis=1, keepdims=True)).astype(jnp.bfloat16)
-    result = lax.dot_general(
-        probabilities, cache[:LATENT, :], (((1,), (1,)), ((), ())),
-        preferred_element_type=jnp.float32,
-    )
-    result = jnp.where(ended[tp] == 0, result, 0.0).astype(jnp.bfloat16)
-    attended[...] = result.reshape(attended.shape)
+
+    def attend(places):
+        query_block = jnp.concatenate([own_queries[place] for place in places], axis=0)
+        scores = jnp.dot(query_block, cache, preferred_element_type=jnp.float32) * score_scale
+        positions = lax.broadcasted_iota(jnp.int32, scores.shape, 1)
+        scores = jnp.where(positions < lengths[tp], scores, -jnp.inf)
+        highest = jnp.max(scores, axis=1, keepdims=True)
+        exps = jnp.exp(scores - highest)
+        probabilities = (exps / jnp.sum(exps, axis=1, keepdims=True)).astype(jnp.bfloat16)
+        result = lax.dot_general(
+            probabilities, cache[:LATENT, :], (((1,), (1,)), ((), ())),
+            preferred_element_type=jnp.float32,
+        )
+        result = jnp.where(ended[tp] == 0, result, 0.0).astype(jnp.bfloat16)
+        for i, place in enumerate(places):
+            attended[place] = result[i * heads : (i + 1) * heads]
 
     def context_to(k):
         target = forth(tp, slots, k)
@@ -374,7 +375,12 @@
             "tp", target,
         )
 
-    for k in hops(slots):
+    far_places, near_places = hops(slots)[: slots - slots // 2], hops(slots)[slots - slots // 2 :]
+    attend([forth(tp, slots, k) for k in far_places])
+    for k in far_places:
+        context_to(k).start()
+    attend([forth(tp, slots, k) for k in near_places] + [tp])
+    for k in near_places:
         context_to(k).start()
     own_context = pltpu.make_async_copy(attended.at[tp], context.at[tp], local_sem.at[5])
     own_context.start()
@@ -456,8 +462,9 @@
     heads = queries.shape[1] // latent_width
     width = moe_input.shape[1]
     chunk = -(-(latent_width // replicas) // PACK) * PACK
-    piece = chunk // PIECES if chunk % (PIECES * PACK) == 0 else chunk
-    pieces = chunk // piece
+    units = chunk // PACK
+    piece = [PACK * u for u in (units // 4, units // 3, units - units // 3 - units // 4) if u]
+    pieces = len(piece)
     everyone = replicas * slots
     bf16, f32 = jnp.bfloat16, jnp.float32
     dma = pltpu.SemaphoreType.DMA
@@ -485,7 +492,7 @@
             pltpu.VMEM((replicas, slots, width + LANES), bf16),
             pltpu.VMEM((everyone, width + LANES), f32),
             pltpu.VMEM((slots, everyone, width), bf16),
-            [pltpu.VMEM((replicas, piece, length), bf16)] * pieces,
+            [pltpu.VMEM((replicas, rows, length), bf16) for rows in piece],
             pltpu.VMEM((replicas, chunk, length), bf16),
             pltpu.VMEM((latent_width, length), bf16),
             pltpu.VMEM(queries.shape, bf16),

time: 40.3 us -> 40.1 us (level)
  no operation moved by 1% of the time
where the time goes in v6:
time: 40.1 us; the launch traced here: 39.9 us
  Pallas kernels  39.2 us (98%)
  between operations  0.64 us (2%)
    pallas_call x1, Pallas kernels, shards(): pl.pallas_call(functools.partial(layer_kernel, replicas, slots, chunk, pi...  37.2 us
    pallas_call x1, Pallas kernels, shards(): pl.pallas_call(write_kernel, out_shape=(jax.ShapeDtypeStruct((latent_widt...  2.02 us

profile of v6, /device:TPU:0, one launch (start us, length us, event | category | flops | bytes accessed | tf_op | source)
XLA Modules:
  0.0 39.9 jit_solution(15517507634509623231)
XLA Ops:
  0.6 37.2 %shard_map.121 = (bf16[576,512]{1,0:T(8,128)(2,1)}, bf16[4,32,512]{2,1,0:T(8,128)(2,1)}, bf16[4,1792]{1,0:T(4,128)(2,1)}) custom-call(s32[4,4]{1,0:T(4,128)} %destination.1, s32[4]{0:T(128)} %cache_len.1, s32[4]{0:T(128)} %finished.1, bf16[576,512]{1,0:T(8,128)(2,1)} %bitcast.2, bf16[4,18432]{1,0:T(4,128)(2,1)} %queries.1, bf16[4,1792]{1,0:T(4,128)(2,1)} %moe_input.1, ...), custom_call_target="tpu_custom_call" | custom-call | tf_op jit(solution)/shard_map/pallas_call | solution.py:473
  37.8 2.0 %shard_map.122 = (bf16[576,512]{1,0:T(8,128)(2,1)}, bf16[4,16384]{1,0:T(4,128)(2,1)}, bf16[4,1792]{1,0:T(4,128)(2,1)}) custom-call(bf16[576,512]{1,0:T(8,128)(2,1)} %get-tuple-element.9.moved, bf16[4,32,512]{2,1,0:T(8,128)(2,1)} %get-tuple-element.10.attended, bf16[4,1792]{1,0:T(4,128)(2,1)} %get-tuple-element.11.moe), custom_call_target="tpu_custom_call" | custom-call | tf_op jit(solution)/shard_map/pallas_call | solution.py:543
